TPU v7x, 128 devices: a whole 4x4x4 slice. The times are simulated.
128 devices in a mesh: blk: 4 (over y_hi, core), ga: 32 (over x, y_lo, z).
Axes of the slice: x: 4, y: 4 (y_hi: 2, y_lo: 2; y = y_hi * 2 + y_lo), z: 4, core: 2. Of those that a mesh axis runs over, the one named last changes fastest.
Arguments:
- screening: bfloat16 [16384, 16384], P('ga', 'blk'), as said below
- pair_elements: bfloat16 [16384, 2048], P('ga', 'blk'), may hold values from -6 to 6
- summed_bands: int32 [16], P('blk'), may hold values from 0 to 2047
- occupied: int32 [1], replicated, may hold values from 768 to 1280
Outputs:
- sigma: float32 [128, 128], P(('blk', 'ga'))
Inputs may be any that keep to these rules, and one draw needn't show every extreme that they name: screening is symmetric: screening[G, G'] = screening[G', G]; its diagonal lies between 0.3 and 3 and its off-diagonal entries have magnitude at most 4 / sqrt(16384).
All inputs are finite; a program needn't handle non-finite values.
Results may differ from a plain program's by a relative error of at most 0.0017.
Values may be sent and summed in bfloat16 or wider, within the bound.
No kernel may reach another device: no remote copies, remote signals or barrier semaphores. Data moves between devices by JAX's collectives and lax.ppermute only.
A program may use at most 128 MiB of HBM per device.

v0:
```python
import math

import jax
import jax.numpy as jnp
from jax import lax
from jax.sharding import PartitionSpec as P

NS = 128


def shards(screening, pair_elements, summed_bands, occupied):
    local_rows = pair_elements.shape[0]
    block_count = lax.axis_size("blk")
    total_g = local_rows * lax.axis_size("ga")
    band_count = summed_bands.shape[0]
    weight = jnp.where(summed_bands < occupied[0], -0.5, 0.5).astype(jnp.float32)
    scale = 1.0 / math.sqrt(total_g * band_count * block_count)
    all_rows = lax.all_gather(pair_elements, "ga", axis=0, tiled=True)
    elements = pair_elements.reshape(local_rows, band_count, NS)
    screened = jnp.dot(
        lax.all_gather(screening, "blk", axis=1, tiled=True),
        all_rows,
        preferred_element_type=jnp.float32,
    )
    weighted = (screened.reshape(local_rows, band_count, NS) * weight[None, :, None]).astype(
        jnp.bfloat16
    )
    partial_value = jnp.einsum(
        "gmn,gmk->nk", elements, weighted, preferred_element_type=jnp.float32
    )
    partial_value = partial_value * jnp.float32(scale)
    return lax.psum_scatter(partial_value, ("blk", "ga"), scatter_dimension=0, tiled=True)


def solution(mesh):
    placed = (P("ga", "blk"), P("ga", "blk"), P("blk"), P())
    return jax.shard_map(
        shards, mesh=mesh, in_specs=placed, out_specs=P(("blk", "ga"), None), check_vma=False
    )
```

profile of v0, /device:TPU:1, one launch (start us, length us, event | category | flops | bytes accessed | tf_op | source)
XLA Modules:
  0.0 476.5 jit_solution(7233950195198310115)
XLA Ops:
  6.5 0.0 all-gather.3.cloned.1.call-start
  6.5 0.7 all-gather.3.cloned.1.call-update
  7.3 0.0 all-gather.5.cloned.1.call-start
  7.3 0.7 all-gather.5.cloned.1.call-update
  8.0 0.0 all-reduce.3.cloned.1.call-start
  8.7 0.7 compare_select_fusion
  9.4 0.1 broadcast_bitcast_fusion
  9.4 0.0 copy-start
  9.4 113.2 %all-gather.3.cloned.1.call-done = bf16[512,16384]{1,0:T(8,128)(2,1)} async-done(((bf16[512,4096]{1,0:T(8,128)(2,1)}), bf16[512,16384]{1,0:T(8,128)(2,1)}) %all-gather.3.cloned.1.call-update) | async-done | bytes 16777232 | tf_op jit(solution)/shard_map/all_gather | solution.py:21
  122.7 188.3 %all-gather.5.cloned.1.call-done = bf16[16384,512]{1,0:T(8,128)(2,1)} async-done(((bf16[512,512]{1,0:T(8,128)(2,1)}), bf16[16384,512]{1,0:T(8,128)(2,1)}) %all-gather.5.cloned.1.call-update) | async-done | bytes 16777232 | tf_op jit(solution)/shard_map/all_gather | solution.py:18
  310.9 14.9 %fusion = bf16[512,512]{0,1:T(8,128)(2,1)S(1)} fusion(bf16[512,16384]{1,0:T(8,128)(2,1)} %all-gather.3.cloned.1.call-done, bf16[16384,512]{1,0:T(8,128)(2,1)} %all-gather.5.cloned.1.call-done, f32[512]{0:T(512)S(1)} %broadcast_bitcast_fusion), kind=kOutput, calls=%fused_computation.1 | convolution fusion | flops 8590458880 | bytes 34080768 | tf_op jit(solution)/shard_map/dot_general | solution.py:20
  325.9 0.0 copy-done
  325.9 0.9 fusion.2
  326.8 0.0 all-reduce.3.cloned.1.call-update
  326.8 141.6 %all-reduce.3.cloned.1.call-done = f32[128,128]{0,1:T(8,128)} async-done(((f32[128,128]{0,1:T(8,128)}), f32[128,128]{0,1:T(8,128)}) %all-reduce.3.cloned.1.call-update) | async-done | bytes 65552
  468.4 0.9 constant_dynamic-slice_fusion
  469.3 0.6 copy.8
Async XLA Ops:
  6.5 116.1 %all-gather.3.cloned.1.call-start = ((), (), s32[]{:S(2)}) async-start(), calls=%async_computation | async-start | bytes 20971520 | tf_op jit(solution)/shard_map/all_gather | solution.py:21
  7.3 303.7 %all-gather.5.cloned.1.call-start = ((), (), s32[]{:S(2)}) async-start(), calls=%async_computation.1 | async-start | bytes 17301504 | tf_op jit(solution)/shard_map/all_gather | solution.py:18
  8.0 460.4 %all-reduce.3.cloned.1.call-start = ((), (), s32[]{:S(2)}) async-start(), calls=%async_computation.2 | async-start | bytes 131072
  9.4 316.4 %copy-start = (bf16[512,512]{1,0:T(8,128)(2,1)S(1)}, bf16[512,512]{1,0:T(8,128)(2,1)}, u32[]{:S(2)}) copy-start(bf16[512,512]{1,0:T(8,128)(2,1)} %param.5) | copy-start | bytes 1572868
Sparse Core Ops, SparseCore 0:
  9.0 113.6 all-gather.2
  124.3 186.5 all-gather.4
  326.9 141.4 all-reduce.2
where the time goes:
time: 477 us; the launch traced here: 476 us
  waiting for transfers between devices  445 us (93%)
  matrix products  15.8 us (3%)
  between operations  13.8 us (3%)
    all_gather x1, waiting for transfers between devices, shards(): all_rows = lax.all_gather(pair_elements, 'ga', axis=0, tiled=True)  188 us
    unnamed x4, waiting for transfers between devices  143 us
    all_gather x1, waiting for transfers between devices, shards(): lax.all_gather(screening, 'blk', axis=1, tiled=True)  113 us
    dot_general x1, matrix products, shards(): jnp.dot(lax.all_gather(screening, 'blk', axis=1, tiled=True), all_rows, p...  14.9 us
  transfers between devices with their start and end apart: 3, of which 3 were waited for; matrix products, arithmetic and copies ran while one was open for 0% of the time, Pallas kernels for 0%

commit v1 on v0

v1 whole, which is shorter than its diff:
```python
import math

import jax
import jax.numpy as jnp
from jax import lax
from jax.experimental import pallas as pl
from jax.experimental.pallas import tpu as pltpu
from jax.sharding import PartitionSpec as P

NS = 128
AXES = ("blk", "ga")


def place(x, y, z, core):
    return ((y // 2) * 2 + core) * 32 + (x % 4) * 8 + (y % 2) * 4 + z % 4


def pairs(target, keep=lambda x, y, z, core: True):
    return [
        (place(x, y, z, core), place(*target(x, y, z, core)))
        for x in range(4)
        for y in range(4)
        for z in range(4)
        for core in range(2)
        if keep(x, y, z, core)
    ]


def inner(x, y):
    return x // 2 == y // 2


def far_core(x, y):
    return 1 - (x if inner(x, y) else 3 - x) % 2


def is_inner(x, y, z, core):
    return inner(x, y)


def is_far(x, y, z, core):
    return core == far_core(x, y)


def to_near_plane(x, y, z, core):
    return (3 - x, y, z, core) if inner(x, y) else (x, (y + 2) % 4, z, core)


def to_partner(x, y, z, core):
    return x ^ 1, y, z, far_core(x ^ 1, y)


CORE_NEAR = pairs(
    lambda x, y, z, core: (x, y, z, 1 - core), lambda x, y, z, core: not is_far(x, y, z, core)
)
CORE_FAR = pairs(lambda x, y, z, core: (x, y, z, 1 - core), is_far)
INJECT = pairs(to_near_plane)
RETURN = pairs(to_near_plane, lambda x, y, z, core: not inner(x, y))
SWAP = pairs(to_partner, is_far)
PARTNER = pairs(lambda x, y, z, core: (x ^ 1, y, z, core))
SIDE = pairs(lambda x, y, z, core: (x, y ^ 1, z, core))
SIDE_INNER = pairs(lambda x, y, z, core: (x, y ^ 1, z, core), is_inner)


def down(x, y, z, core):
    return x, y, z - 1, core


def up(x, y, z, core):
    return x, y, z + 1, core


DOWN, UP = pairs(down), pairs(up)

SLOTS = 9
NEAR, INNER, SIDE_OWN = range(SLOTS, SLOTS + 3)


def send(value, table):
    return lax.ppermute(value, AXES, table)


def blend(flag, yes, no):
    flag = flag.astype(yes.dtype)
    return yes * flag + no * (1 - flag)


def products(table, factors, near, far, weight_b, blocks, before=None, scale=None):
    (near_w, *near_rows), (far_w, *far_rows) = near, far
    parts = [len(near_w), len(far_w)]
    rows, (depth, width) = sum(part.shape[0] for part in near_w), blocks[0].shape
    bands = width // NS

    def kernel(table, factors, *refs):
        near_refs, refs = refs[: parts[0]], refs[parts[0] :]
        far_refs, refs = refs[: parts[1]], refs[parts[1] :]
        near_a, near_b, far_a, far_b, weight_ref = refs[:5]
        own, brought, own_side, brought_side, up_1, down_1, up_2, down_2 = refs[5:13]
        across_up, across_down = refs[13:15]
        refs = refs[15:]
        if before is not None:
            before_ref, refs = refs[0], refs[1:]
        out, w, q, left, sems = refs

        def choose(flag, yes, no):
            if yes is no:
                copy(*yes)
                return

            @pl.when(table[flag] == 1)
            def _():
                copy(*yes)

            @pl.when(table[flag] == 0)
            def _():
                copy(*no)

        def copy(*triples):
            for source, target, sem in triples:
                pltpu.make_async_copy(source, target, sem).start()

        def part(slot):
            return slot // 4, pl.ds((slot % 4) * depth, depth)

        sources = [
            (INNER, own, brought),
            (INNER, up_1, up_1),
            (INNER, up_2, up_2),
            (INNER, across_up, across_up),
            (INNER, brought, brought),
            (INNER, down_1, down_1),
            (INNER, down_2, down_2),
            (INNER, across_down, across_down),
            (SIDE_OWN, own_side, brought_side),
        ]
        for slot in (8, 0, 1, 2, 3, 4, 5, 6, 7):
            flag, yes, no = sources[slot]
            yes, no = yes.at[pl.ds(0, depth)], no.at[pl.ds(0, depth)] if no is not yes else None
            group, place_in = part(slot)
            target, sem = q.at[group, place_in], sems.at[0, group]
            if no is None:
                copy((yes, target, sem))
            else:
                choose(flag, [(yes, target, sem)], [(no, target, sem)])
            columns = pl.ds(pl.multiple_of(table[slot] * depth, depth), depth)
            copies = []
            for side in (near_refs, far_refs):
                at, triples = 0, []
                for ref in side:
                    target = w.at[group, pl.ds(at, ref.shape[0]), place_in]
                    triples.append((ref.at[:, columns], target, sems.at[1, group]))
                    at += ref.shape[0]
                copies.append(triples)
            choose(NEAR, *copies)
        block = pl.ds(0, rows)
        targets = [(left.at[group], sems.at[group, 3]) for group in range(2)]
        choose(
            NEAR,
            [(near_a.at[block], *targets[0]), (near_b.at[block], *targets[1])],
            [(far_a.at[block], *targets[0]), (far_b.at[block], *targets[1])],
        )

        def wait(ref, sem):
            pltpu.make_async_copy(ref, ref, sem).wait()

        wait(q.at[2, pl.ds(0, depth)], sems.at[0, 2])
        wait(w.at[2, :, pl.ds(0, depth)], sems.at[1, 2])
        side = jnp.dot(w[2, :, :depth], q[2, :depth], preferred_element_type=jnp.float32)
        result = jnp.zeros((NS, 2 * NS), jnp.float32)
        for group in range(2):
            wait(q.at[group], sems.at[0, group])
            wait(w.at[group], sems.at[1, group])
            q[group, :depth] = q[group, :depth] * factors[group].astype(q.dtype)
            total = jnp.dot(w[group], q[group], preferred_element_type=jnp.float32)
            total = total + side * factors[2 + group]
            if group == 1:
                total = total * weight_ref[0:1, :].astype(jnp.float32)
            high = total.astype(jnp.bfloat16)
            low = (total - high.astype(jnp.float32)).astype(jnp.bfloat16)
            wait(left.at[group], sems.at[group, 3])
            for band in range(bands):
                lanes = slice(band * NS, (band + 1) * NS)
                result = result + lax.dot_general(
                    left[group, :, lanes],
                    jnp.concatenate([high[:, lanes], low[:, lanes]], 1),
                    (((0,), (0,)), ((), ())),
                    preferred_element_type=jnp.float32,
                )
        result = result[:, :NS] + result[:, NS:]
        if before is not None:
            result = result + before_ref[...]
            result = (result + result.T) * jnp.float32(scale)
        out[...] = result

    hbm = pl.BlockSpec(memory_space=pl.ANY)
    vmem = pl.BlockSpec(memory_space=pltpu.VMEM)
    smem = pl.BlockSpec(memory_space=pltpu.SMEM)
    more = [] if before is None else [before]
    return pl.pallas_call(
        kernel,
        out_shape=jax.ShapeDtypeStruct((NS, NS), jnp.float32),
        in_specs=[smem, smem] + [hbm] * (sum(parts) + 4) + [vmem] + [hbm] * 10 + [vmem] * len(more),
        out_specs=vmem,
        scratch_shapes=[
            pltpu.VMEM((3, rows, 4 * depth), jnp.bfloat16),
            pltpu.VMEM((3, 4 * depth, width), jnp.bfloat16),
            pltpu.VMEM((2, rows, width), jnp.bfloat16),
            pltpu.SemaphoreType.DMA((2, 4)),
        ],
        compiler_params=pltpu.CompilerParams(vmem_limit_bytes=60 * 1024 * 1024),
        cost_estimate=pl.CostEstimate(
            flops=2 * SLOTS * rows * depth * width,
            bytes_accessed=2 * SLOTS * (rows + width) * depth,
            transcendentals=0,
        ),
    )(table, factors, *near_w, *far_w, *near_rows, *far_rows, weight_b, *blocks, *more)


def shards(screening, pair_elements, summed_bands, occupied):
    rows = pair_elements.shape[0]
    bands = summed_bands.shape[0]
    total_g = rows * lax.axis_size("ga")
    scale = 1.0 / math.sqrt(total_g * bands * lax.axis_size("blk"))
    blk, ga = lax.axis_index("blk"), lax.axis_index("ga")
    y_hi, core = blk // 2, blk % 2
    x, y_lo, z = ga // 8, (ga // 4) % 2, ga % 4
    at_inner = x // 2 == y_hi
    near_plane = jnp.where(at_inner, x, 3 - x)
    near = core == near_plane % 2

    low, first = z < 2, y_lo == 0
    other = 1 - y_lo
    z_up, z_down, z_across = (z + 1) % 4, (z + 3) % 4, (z + 2) % 4
    table = [y_lo * 4 + z, y_lo * 4 + z_up, other * 4 + z_up]
    table += [jnp.where(low, y_lo, other) * 4 + z_across]
    table += [y_lo * 4 + z, y_lo * 4 + z_down, other * 4 + z_down]
    table += [jnp.where(low, other, y_lo) * 4 + z_across, other * 4 + z]
    table += [near, at_inner, at_inner & first]
    table = jnp.stack([entry.astype(jnp.int32) for entry in table])
    odd = x % 2
    sides = [first, ~first]
    factors_own = [jnp.where(at_inner, 0.5, 1.0), jnp.where(at_inner, 0.5, 0.0)] + sides
    factors_partner = [jnp.where(at_inner, odd, 1), jnp.where(at_inner, 1 - odd, 0)] + sides
    factors_own = jnp.stack([entry * jnp.float32(1) for entry in factors_own])
    factors_partner = jnp.stack([entry * jnp.float32(1) for entry in factors_partner])
    factors_here = jnp.where(near, factors_own, factors_partner)
    factors_there = jnp.where(near, factors_partner, factors_own)
    one = jnp.ones((1, bands * NS), pair_elements.dtype)
    weight = jnp.where(summed_bands < occupied[0], -0.5, 0.5).astype(pair_elements.dtype)
    weight = jnp.broadcast_to(jnp.repeat(weight, NS)[None, :], (16, bands * NS))

    held = lax.optimization_barrier
    own = pair_elements
    cut = rows * 11 // 16
    brought = send(jnp.concatenate([own, weight], 0), INJECT)
    own_side = send(own, SIDE_INNER)
    own_rows = own * weight[:1]
    partner_rows = send(own_rows, PARTNER)
    (
        brought, own_side, own_rows, partner_rows, far_1, far_2, table, factors_here, factors_there, one,
    ) = held(
        (
            brought, own_side, own_rows, partner_rows, screening[:cut], screening[cut:],
            table, factors_here, factors_there, one,
        )
    )

    swapped_1 = send(far_1, SWAP)
    brought_side = send(brought, SIDE)
    up_1 = send(blend(at_inner, own, brought[:rows]), DOWN)
    down_1 = send(brought, UP)
    native_side = blend(at_inner, own_side, brought_side[:rows])
    own_side, brought, brought_side, native_side, up_1, down_1, partner_rows = held(
        (own_side, brought, brought_side, native_side, up_1, down_1, partner_rows)
    )

    up_2 = send(native_side, DOWN)
    down_2 = send(brought_side, UP)
    foreign_rows = send(partner_rows, RETURN)
    brought_weight = jnp.where(at_inner, brought[rows : rows + 1], one)
    weight_here = jnp.where(near, brought_weight, one)
    weight_there = jnp.where(near, one, brought_weight)
    foreign_own = blend(at_inner, brought[:rows], own_rows)
    (
        swapped_1, foreign_rows, up_1, down_1, up_2, down_2, far_2,
        weight_here, weight_there, foreign_own,
    ) = held(
        (
            swapped_1, foreign_rows, up_1, down_1, up_2, down_2, far_2,
            weight_here, weight_there, foreign_own,
        )
    )

    swapped_2 = send(far_2, SWAP)
    across_up = send(blend((z + 3) % 4 < 2, up_1, up_2), DOWN)
    across_down = send(blend((z + 1) % 4 < 2, down_2, down_1), UP)
    foreign_partner = blend(at_inner, foreign_rows, partner_rows)
    swapped_1, swapped_2, across_up, across_down, near_w, foreign_partner = held(
        (swapped_1, swapped_2, across_up, across_down, screening, foreign_partner)
    )

    near_other = send(near_w, CORE_NEAR)
    swapped_other = [send(swapped_1, CORE_FAR), send(swapped_2, CORE_FAR)]
    blocks = [own, brought, own_side, brought_side, up_1, down_1, up_2, down_2]
    blocks += [across_up, across_down]
    half = products(
        table,
        factors_here,
        ([near_w], own_rows, foreign_own),
        ([swapped_1, swapped_2], partner_rows, foreign_partner),
        weight_here,
        blocks,
    )
    value = products(
        table,
        factors_there,
        (swapped_other, partner_rows, foreign_partner),
        ([near_other], own_rows, foreign_own),
        weight_there,
        blocks,
        half,
        scale,
    )
    parts = lax.all_to_all(value.reshape(NS, 1, NS), AXES, 0, 0)
    return jnp.sum(parts, 0)


def solution(mesh):
    placed = (P("ga", "blk"), P("ga", "blk"), P("blk"), P())
    return jax.shard_map(
        shards, mesh=mesh, in_specs=placed, out_specs=P(("blk", "ga"), None), check_vma=False
    )
```

time: 477 us -> 123 us (0.26)
  waiting for transfers between devices: 445 us -> 41.4 us
  starting transfers between devices: 0.08 us -> 35.1 us
  matrix products: 15.8 us -> 0 us
  Pallas kernels: 0 us -> 15 us
  blocking collectives: 0 us -> 14.3 us
  between operations: 13.8 us -> 1.18 us
  local copies, waits for them, and re-layouts: 1.58 us -> 9.35 us
  other arithmetic: 0.66 us -> 6.12 us
    all_gather x2 -> x0, waiting for transfers between devices: 301 us -> none  [the longest x1 188 us: shards(): all_rows = lax.all_gather(pair_elements, 'ga', axis=0, tiled=True)]
    unnamed x4 -> x0, waiting for transfers between devices: 143 us -> none
    ppermute x0 -> x16, waiting for transfers between devices: none -> 41.4 us  [send(): return lax.ppermute(value, AXES, table)]
    ppermute x0 -> x16, starting transfers between devices: none -> 35.1 us  [send(): return lax.ppermute(value, AXES, table)]
    dot_general x2 -> x0, matrix products: 15.8 us -> none  [the longest x1 14.9 us: shards(): jnp.dot(lax.all_gather(screening, 'blk', axis=1, tiled=True), all_rows, p...]
    pallas_call x0 -> x2, Pallas kernels: none -> 15 us  [products(): pl.pallas_call(kernel, out_shape=jax.ShapeDtypeStruct((NS, NS), jnp.float...]
    all_to_all x0 -> x1, blocking collectives: none -> 14.3 us  [shards(): parts = lax.all_to_all(value.reshape(NS, 1, NS), AXES, 0, 0)]
    slice x0 -> x2, local copies, waits for them, and re-layouts: none -> 6.21 us  [the longest x1 3.71 us: shards(): screening[:cut]]
  transfers between devices with their start and end apart: 3 -> 16, of which waited for: 3 -> 10; matrix products, arithmetic and copies ran while one was open for 0% -> 9% of each run, Pallas kernels for 0% -> 6%
where the time goes in v1:
time: 123 us
  waiting for transfers between devices  41.4 us (34%)
  starting transfers between devices  35.1 us (29%)
  Pallas kernels  15 us (12%)
  blocking collectives  14.3 us (12%)
  local copies, waits for them, and re-layouts  9.35 us (8%)
  other arithmetic  6.12 us (5%)
    ppermute x16, waiting for transfers between devices, send(): return lax.ppermute(value, AXES, table)  41.4 us
    ppermute x16, starting transfers between devices, send(): return lax.ppermute(value, AXES, table)  35.1 us
    pallas_call x2, Pallas kernels, products(): pl.pallas_call(kernel, out_shape=jax.ShapeDtypeStruct((NS, NS), jnp.float...  15 us
    all_to_all x1, blocking collectives, shards(): parts = lax.all_to_all(value.reshape(NS, 1, NS), AXES, 0, 0)  14.3 us
    slice x1, local copies, waits for them, and re-layouts, shards(): screening[:cut]  3.71 us
    slice x1, local copies, waits for them, and re-layouts, shards(): screening[cut:]  2.5 us
  transfers between devices with their start and end apart: 16, of which 10 were waited for; matrix products, arithmetic and copies ran while one was open for 9% of the time, Pallas kernels for 6%

profile of v1, /device:TPU:1, one launch (start us, length us, event | category | flops | bytes accessed | tf_op | source)
XLA Modules:
  0.0 122.5 jit_solution(16158530157246139175)
XLA Ops:
  2.5 3.4 %collective-permute-start = (bf16[528,512]{1,0:T(8,128)(2,1)S(1)}, bf16[528,512]{1,0:T(8,128)(2,1)S(1)}, u32[]{:S(2)}, u32[]{:S(2)}) collective-permute-start(bf16[528,512]{1,0:T(8,128)(2,1)S(1)} %pad_maximum_fusion), channel_id=1, source_target_pairs={{0,24},{32,56},{1,25},{33,57},{2,26},{34,58},{3,27},{35,59},{4,28}... | collective-permute-start | bytes 1622024 | tf_op jit(solution)/shard_map/ppermute | solution.py:80
  6.1 3.2 %collective-permute-start.1 = (bf16[512,512]{1,0:T(8,128)(2,1)S(1)}, bf16[512,512]{1,0:T(8,128)(2,1)S(1)}, u32[]{:S(2)}, u32[]{:S(2)}) collective-permute-start(bf16[512,512]{1,0:T(8,128)(2,1)S(1)} %copy-done), channel_id=1, source_target_pairs={{0,4},{32,36},{1,5},{33,37},{2,6},{34,38},{3,7},{35,39},{4,0},{36,... | collective-permute-start | bytes 1572872 | tf_op jit(solution)/shard_map/ppermute | solution.py:80
  9.4 2.5 %slice.20 = bf16[160,4096]{1,0:T(8,128)(2,1)} slice(bf16[512,4096]{1,0:T(8,128)(2,1)} %refs_0_), slice={[352:512], [0:4096]} | slice | bytes 2621440 | tf_op jit(solution)/shard_map/slice | solution.py:263
  11.9 3.7 %slice.19 = bf16[352,4096]{1,0:T(8,128)(2,1)} slice(bf16[512,4096]{1,0:T(8,128)(2,1)} %refs_0_), slice={[0:352], [0:4096]} | slice | bytes 5767168 | tf_op jit(solution)/shard_map/slice | solution.py:263
  18.5 1.7 %collective-permute-done.1.refs_10_ = bf16[512,512]{1,0:T(8,128)(2,1)S(1)} collective-permute-done((bf16[512,512]{1,0:T(8,128)(2,1)S(1)}, bf16[512,512]{1,0:T(8,128)(2,1)S(1)}, u32[]{:S(2)}, u32[]{:S(2)}) %collective-permute-start.1) | collective-permute-done | bytes 524320 | tf_op jit(solution)/shard_map/ppermute | solution.py:80
  20.2 5.3 %collective-permute-start.3 = (bf16[352,4096]{1,0:T(8,128)(2,1)}, bf16[352,4096]{1,0:T(8,128)(2,1)}, u32[]{:S(2)}, u32[]{:S(2)}) collective-permute-start(bf16[352,4096]{1,0:T(8,128)(2,1)} %slice.19), channel_id=1, source_target_pairs={{32,8},{33,9},{34,10},{35,11},{36,12},{37,13},{38,14},{39,15},{64,... | collective-permute-start | bytes 8650760 | tf_op jit(solution)/shard_map/ppermute | solution.py:80
  25.5 1.4 %collective-permute-start.4 = (bf16[528,512]{1,0:T(8,128)(2,1)S(1)}, bf16[528,512]{1,0:T(8,128)(2,1)S(1)}, u32[]{:S(2)}, u32[]{:S(2)}) collective-permute-start(bf16[528,512]{1,0:T(8,128)(2,1)S(1)} %collective-permute-done.refs_9_), channel_id=1, source_target_pairs={{0,4},{32,36},{1,5},{33,37},{2,6},{34,38},{3,7},{35,39},{4,0},{36,... | collective-permute-start | bytes 1622024 | tf_op jit(solution)/shard_map/ppermute | solution.py:80
  26.9 1.6 %collective-permute-start.6 = (bf16[528,512]{1,0:T(8,128)(2,1)S(1)}, bf16[528,512]{1,0:T(8,128)(2,1)S(1)}, u32[]{:S(2)}, u32[]{:S(2)}) collective-permute-start(bf16[528,512]{1,0:T(8,128)(2,1)S(1)} %collective-permute-done.refs_9_), channel_id=1, source_target_pairs={{0,1},{32,33},{1,2},{33,34},{2,3},{34,35},{3,0},{35,32},{4,5},{36,... | collective-permute-start | bytes 1622024 | tf_op jit(solution)/shard_map/ppermute | solution.py:80
  28.6 2.2 %collective-permute-start.5 = (bf16[512,512]{1,0:T(8,128)(2,1)S(1)}, bf16[512,512]{1,0:T(8,128)(2,1)S(1)}, u32[]{:S(2)}, u32[]{:S(2)}) collective-permute-start(bf16[512,512]{1,0:T(8,128)(2,1)S(1)} %multiply_add_fusion.4), channel_id=1, source_target_pairs={{0,3},{32,35},{1,0},{33,32},{2,1},{34,33},{3,2},{35,34},{4,7},{36,... | collective-permute-start | bytes 1572872 | tf_op jit(solution)/shard_map/ppermute | solution.py:80
  30.8 8.5 %collective-permute-done.4.refs_11_ = bf16[528,512]{1,0:T(8,128)(2,1)S(1)} collective-permute-done((bf16[528,512]{1,0:T(8,128)(2,1)S(1)}, bf16[528,512]{1,0:T(8,128)(2,1)S(1)}, u32[]{:S(2)}, u32[]{:S(2)}) %collective-permute-start.4) | collective-permute-done | bytes 540704 | tf_op jit(solution)/shard_map/ppermute | solution.py:80
  39.4 3.0 %collective-permute-done.5.refs_12_ = bf16[512,512]{1,0:T(8,128)(2,1)S(1)} collective-permute-done((bf16[512,512]{1,0:T(8,128)(2,1)S(1)}, bf16[512,512]{1,0:T(8,128)(2,1)S(1)}, u32[]{:S(2)}, u32[]{:S(2)}) %collective-permute-start.5) | collective-permute-done | bytes 524320 | tf_op jit(solution)/shard_map/ppermute | solution.py:80
  42.6 1.7 %collective-permute-start.9 = (bf16[528,512]{1,0:T(8,128)(2,1)S(1)}, bf16[528,512]{1,0:T(8,128)(2,1)S(1)}, u32[]{:S(2)}, u32[]{:S(2)}) collective-permute-start(bf16[528,512]{1,0:T(8,128)(2,1)S(1)} %collective-permute-done.4.refs_11_), channel_id=1, source_target_pairs={{0,1},{32,33},{1,2},{33,34},{2,3},{34,35},{3,0},{35,32},{4,5},{36,... | collective-permute-start | bytes 1622024 | tf_op jit(solution)/shard_map/ppermute | solution.py:80
  48.3 8.8 %collective-permute-done.8.refs_14_ = bf16[512,512]{1,0:T(8,128)(2,1)S(1)} collective-permute-done((bf16[512,512]{1,0:T(8,128)(2,1)S(1)}, bf16[512,512]{1,0:T(8,128)(2,1)S(1)}, u32[]{:S(2)}, u32[]{:S(2)}) %collective-permute-start.8) | collective-permute-done | bytes 524320 | tf_op jit(solution)/shard_map/ppermute | solution.py:80
  57.1 4.6 %collective-permute-done.7 = bf16[512,512]{1,0:T(8,128)(2,1)S(1)} collective-permute-done((bf16[512,512]{1,0:T(8,128)(2,1)S(1)}, bf16[512,512]{1,0:T(8,128)(2,1)S(1)}, u32[]{:S(2)}, u32[]{:S(2)}) %collective-permute-start.7) | collective-permute-done | bytes 524320 | tf_op jit(solution)/shard_map/ppermute | solution.py:80
  62.5 2.0 %collective-permute-start.10 = (bf16[160,4096]{1,0:T(8,128)(2,1)}, bf16[160,4096]{1,0:T(8,128)(2,1)}, u32[]{:S(2)}, u32[]{:S(2)}) collective-permute-start(bf16[160,4096]{1,0:T(8,128)(2,1)} %slice.20), channel_id=1, source_target_pairs={{32,8},{33,9},{34,10},{35,11},{36,12},{37,13},{38,14},{39,15},{64,... | collective-permute-start | bytes 3932168 | tf_op jit(solution)/shard_map/ppermute | solution.py:80
  64.9 2.7 %collective-permute-start.11 = (bf16[512,512]{1,0:T(8,128)(2,1)S(1)}, bf16[512,512]{1,0:T(8,128)(2,1)S(1)}, u32[]{:S(2)}, u32[]{:S(2)}) collective-permute-start(bf16[512,512]{1,0:T(8,128)(2,1)S(1)} %multiply_add_fusion.2), channel_id=1, source_target_pairs={{0,3},{32,35},{1,0},{33,32},{2,1},{34,33},{3,2},{35,34},{4,7},{36,... | collective-permute-start | bytes 1572872 | tf_op jit(solution)/shard_map/ppermute | solution.py:80
  68.5 8.8 %collective-permute-done.11.refs_16_ = bf16[512,512]{1,0:T(8,128)(2,1)S(1)} collective-permute-done((bf16[512,512]{1,0:T(8,128)(2,1)S(1)}, bf16[512,512]{1,0:T(8,128)(2,1)S(1)}, u32[]{:S(2)}, u32[]{:S(2)}) %collective-permute-start.11) | collective-permute-done | bytes 524320 | tf_op jit(solution)/shard_map/ppermute | solution.py:80
  78.4 3.5 %collective-permute-done.10.refs_2_ = bf16[160,4096]{1,0:T(8,128)(2,1)} collective-permute-done((bf16[160,4096]{1,0:T(8,128)(2,1)}, bf16[160,4096]{1,0:T(8,128)(2,1)}, u32[]{:S(2)}, u32[]{:S(2)}) %collective-permute-start.10) | collective-permute-done | bytes 1310752 | tf_op jit(solution)/shard_map/ppermute | solution.py:80
  83.2 5.2 %collective-permute-start.13 = (bf16[352,4096]{1,0:T(8,128)(2,1)}, bf16[352,4096]{1,0:T(8,128)(2,1)S(1)}, u32[]{:S(2)}, u32[]{:S(2)}) collective-permute-start(bf16[352,4096]{1,0:T(8,128)(2,1)} %collective-permute-done.3.refs_1_), channel_id=1, source_target_pairs={{32,0},{33,1},{34,2},{35,3},{36,4},{37,5},{38,6},{39,7},{64,96},{6... | collective-permute-start | bytes 8650760 | tf_op jit(solution)/shard_map/ppermute | solution.py:80
  88.4 2.5 %collective-permute-start.14 = (bf16[160,4096]{1,0:T(8,128)(2,1)}, bf16[160,4096]{1,0:T(8,128)(2,1)}, u32[]{:S(2)}, u32[]{:S(2)}) collective-permute-start(bf16[160,4096]{1,0:T(8,128)(2,1)} %collective-permute-done.10.refs_2_), channel_id=1, source_target_pairs={{32,0},{33,1},{34,2},{35,3},{36,4},{37,5},{38,6},{39,7},{64,96},{6... | collective-permute-start | bytes 3932168 | tf_op jit(solution)/shard_map/ppermute | solution.py:80
  90.8 7.5 %shard_map.46.refs_18_ = f32[128,128]{1,0:T(8,128)} custom-call(s32[12]{0:T(128)} %stack.92.table, f32[4]{0:T(128)} %broadcast_select_fusion.4.factors, bf16[512,4096]{1,0:T(8,128)(2,1)} %refs_0_, bf16[352,4096]{1,0:T(8,128)(2,1)} %collective-permute-done.3.refs_1_, bf16[160,4096]{1,0:T(8,128)(2,1)} %collective-permute-done.10.refs_2_, ...), custom_call_target="tpu_custom_call" | custom-call | flops 2415919104 | bytes 9437184 | tf_op jit(solution)/shard_map/pallas_call | solution.py:199
  98.3 1.6 %copy-done.13 = bf16[352,4096]{1,0:T(8,128)(2,1)} copy-done((bf16[352,4096]{1,0:T(8,128)(2,1)}, bf16[352,4096]{1,0:T(8,128)(2,1)S(1)}, u32[]{:S(2)}) %copy-start.13) | copy-done | bytes 2883608
  99.9 7.6 %shard_map.47 = f32[128,128]{1,0:T(8,128)} custom-call(s32[12]{0:T(128)} %stack.92.table, f32[4]{0:T(128)} %get-tuple-element.39.factors, bf16[352,4096]{1,0:T(8,128)(2,1)} %copy-done.13, bf16[160,4096]{1,0:T(8,128)(2,1)} %collective-permute-done.14.refs_1_, bf16[512,4096]{1,0:T(8,128)(2,1)} %collective-permute-done.15.refs_2_, bf16[512,512]{1,0:T(8,128)(2,1)} %copy-done.6, ...), custom_call_target="tpu_custom_call" | custom-call | flops 2415919104 | bytes 9437184 | tf_op jit(solution)/shard_map/pallas_call | solution.py:199
  107.5 14.3 %all_to_all.5 = f32[128,1,128]{2,1,0:T(1,128)S(1)} all-to-all(f32[128,1,128]{2,1,0:T(1,128)} %bitcast.25), channel_id=1, replica_groups=mesh['blk'=4,'ga'=32] {'blk','ga'}, dimensions={0} | all-to-all | bytes 131072 | tf_op jit(solution)/shard_map/all_to_all | solution.py:324
  (66 shorter events, 14.2 us)
Async XLA Ops:
  2.5 17.7 %collective-permute-start = (bf16[528,512]{1,0:T(8,128)(2,1)S(1)}, bf16[528,512]{1,0:T(8,128)(2,1)S(1)}, u32[]{:S(2)}, u32[]{:S(2)}) collective-permute-start(bf16[528,512]{1,0:T(8,128)(2,1)S(1)} %pad_maximum_fusion), channel_id=1, source_target_pairs={{0,24},{32,56},{1,25},{33,57},{2,26},{34,58},{3,27},{35,59},{4,28}... | collective-permute-start | bytes 1622024 | tf_op jit(solution)/shard_map/ppermute | solution.py:80
  6.0 41.5 %copy-start.2 = (bf16[512,512]{1,0:T(8,128)(2,1)}, bf16[512,512]{1,0:T(8,128)(2,1)S(1)}, u32[]{:S(2)}) copy-start(bf16[512,512]{1,0:T(8,128)(2,1)S(1)} %broadcast_multiply_fusion.refs_3_.refs_5_) | copy-start | bytes 1572868
  6.0 12.6 %collective-permute-start.2 = (bf16[512,512]{1,0:T(8,128)(2,1)S(1)}, bf16[512,512]{1,0:T(8,128)(2,1)S(1)}, u32[]{:S(2)}, u32[]{:S(2)}) collective-permute-start(bf16[512,512]{1,0:T(8,128)(2,1)S(1)} %broadcast_multiply_fusion.refs_3_.refs_5_), channel_id=1, source_target_pairs={{0,8},{32,40},{1,9},{33,41},{2,10},{34,42},{3,11},{35,43},{4,12},{... | collective-permute-start | bytes 1572872 | tf_op jit(solution)/shard_map/ppermute | solution.py:80
  6.1 14.2 %collective-permute-start.1 = (bf16[512,512]{1,0:T(8,128)(2,1)S(1)}, bf16[512,512]{1,0:T(8,128)(2,1)S(1)}, u32[]{:S(2)}, u32[]{:S(2)}) collective-permute-start(bf16[512,512]{1,0:T(8,128)(2,1)S(1)} %copy-done), channel_id=1, source_target_pairs={{0,4},{32,36},{1,5},{33,37},{2,6},{34,38},{3,7},{35,39},{4,0},{36,... | collective-permute-start | bytes 1572872 | tf_op jit(solution)/shard_map/ppermute | solution.py:80
  20.2 19.2 %copy-start.9 = (bf16[512,512]{1,0:T(8,128)(2,1)}, bf16[512,512]{1,0:T(8,128)(2,1)S(1)}, u32[]{:S(2)}) copy-start(bf16[512,512]{1,0:T(8,128)(2,1)S(1)} %collective-permute-done.1.refs_10_) | copy-start | bytes 1572868
  20.2 27.2 %copy-start.1 = (bf16[528,512]{1,0:T(8,128)(2,1)}, bf16[528,512]{1,0:T(8,128)(2,1)S(1)}, u32[]{:S(2)}) copy-start(bf16[528,512]{1,0:T(8,128)(2,1)S(1)} %collective-permute-done.refs_9_) | copy-start | bytes 1622020
  20.2 41.5 %collective-permute-start.3 = (bf16[352,4096]{1,0:T(8,128)(2,1)}, bf16[352,4096]{1,0:T(8,128)(2,1)}, u32[]{:S(2)}, u32[]{:S(2)}) collective-permute-start(bf16[352,4096]{1,0:T(8,128)(2,1)} %slice.19), channel_id=1, source_target_pairs={{32,8},{33,9},{34,10},{35,11},{36,12},{37,13},{38,14},{39,15},{64,... | collective-permute-start | bytes 8650760 | tf_op jit(solution)/shard_map/ppermute | solution.py:80
  25.5 13.8 %collective-permute-start.4 = (bf16[528,512]{1,0:T(8,128)(2,1)S(1)}, bf16[528,512]{1,0:T(8,128)(2,1)S(1)}, u32[]{:S(2)}, u32[]{:S(2)}) collective-permute-start(bf16[528,512]{1,0:T(8,128)(2,1)S(1)} %collective-permute-done.refs_9_), channel_id=1, source_target_pairs={{0,4},{32,36},{1,5},{33,37},{2,6},{34,38},{3,7},{35,39},{4,0},{36,... | collective-permute-start | bytes 1622024 | tf_op jit(solution)/shard_map/ppermute | solution.py:80
  26.9 18.6 %copy-start.7 = (bf16[512,512]{1,0:T(8,128)(2,1)S(1)}, bf16[512,512]{1,0:T(8,128)(2,1)}, u32[]{:S(2)}) copy-start(bf16[512,512]{1,0:T(8,128)(2,1)} %copy-done.6) | copy-start | bytes 1572868
  26.9 15.7 %collective-permute-start.6 = (bf16[528,512]{1,0:T(8,128)(2,1)S(1)}, bf16[528,512]{1,0:T(8,128)(2,1)S(1)}, u32[]{:S(2)}, u32[]{:S(2)}) collective-permute-start(bf16[528,512]{1,0:T(8,128)(2,1)S(1)} %collective-permute-done.refs_9_), channel_id=1, source_target_pairs={{0,1},{32,33},{1,2},{33,34},{2,3},{34,35},{3,0},{35,32},{4,5},{36,... | collective-permute-start | bytes 1622024 | tf_op jit(solution)/shard_map/ppermute | solution.py:80
  28.6 13.8 %collective-permute-start.5 = (bf16[512,512]{1,0:T(8,128)(2,1)S(1)}, bf16[512,512]{1,0:T(8,128)(2,1)S(1)}, u32[]{:S(2)}, u32[]{:S(2)}) collective-permute-start(bf16[512,512]{1,0:T(8,128)(2,1)S(1)} %multiply_add_fusion.4), channel_id=1, source_target_pairs={{0,3},{32,35},{1,0},{33,32},{2,1},{34,33},{3,2},{35,34},{4,7},{36,... | collective-permute-start | bytes 1572872 | tf_op jit(solution)/shard_map/ppermute | solution.py:80
  39.3 9.0 %copy-start.5 = (bf16[528,512]{1,0:T(8,128)(2,1)}, bf16[528,512]{1,0:T(8,128)(2,1)S(1)}, u32[]{:S(2)}) copy-start(bf16[528,512]{1,0:T(8,128)(2,1)S(1)} %collective-permute-done.4.refs_11_) | copy-start | bytes 1622020
  42.4 22.4 %copy-start.10 = (bf16[512,512]{1,0:T(8,128)(2,1)}, bf16[512,512]{1,0:T(8,128)(2,1)S(1)}, u32[]{:S(2)}) copy-start(bf16[512,512]{1,0:T(8,128)(2,1)S(1)} %collective-permute-done.5.refs_12_) | copy-start | bytes 1572868
  42.6 22.1 %copy-start.3 = (bf16[528,512]{1,0:T(8,128)(2,1)}, bf16[528,512]{1,0:T(8,128)(2,1)S(1)}, u32[]{:S(2)}) copy-start(bf16[528,512]{1,0:T(8,128)(2,1)S(1)} %collective-permute-done.6.refs_13_) | copy-start | bytes 1622020
  42.6 19.1 %collective-permute-start.9 = (bf16[528,512]{1,0:T(8,128)(2,1)S(1)}, bf16[528,512]{1,0:T(8,128)(2,1)S(1)}, u32[]{:S(2)}, u32[]{:S(2)}) collective-permute-start(bf16[528,512]{1,0:T(8,128)(2,1)S(1)} %collective-permute-done.4.refs_11_), channel_id=1, source_target_pairs={{0,1},{32,33},{1,2},{33,34},{2,3},{34,35},{3,0},{35,32},{4,5},{36,... | collective-permute-start | bytes 1622024 | tf_op jit(solution)/shard_map/ppermute | solution.py:80
  44.3 12.8 %collective-permute-start.8 = (bf16[512,512]{1,0:T(8,128)(2,1)S(1)}, bf16[512,512]{1,0:T(8,128)(2,1)S(1)}, u32[]{:S(2)}, u32[]{:S(2)}) collective-permute-start(bf16[512,512]{1,0:T(8,128)(2,1)S(1)} %fusion), channel_id=1, source_target_pairs={{0,3},{32,35},{1,0},{33,32},{2,1},{34,33},{3,2},{35,34},{4,7},{36,... | collective-permute-start | bytes 1572872 | tf_op jit(solution)/shard_map/ppermute | solution.py:80
  45.5 16.2 %collective-permute-start.7 = (bf16[512,512]{1,0:T(8,128)(2,1)S(1)}, bf16[512,512]{1,0:T(8,128)(2,1)S(1)}, u32[]{:S(2)}, u32[]{:S(2)}) collective-permute-start(bf16[512,512]{1,0:T(8,128)(2,1)S(1)} %copy-done.7), channel_id=1, source_target_pairs={{64,0},{96,32},{65,1},{97,33},{66,2},{98,34},{67,3},{99,35},{68,4}... | collective-permute-start | bytes 1572872 | tf_op jit(solution)/shard_map/ppermute | solution.py:80
  62.5 19.4 %collective-permute-start.10 = (bf16[160,4096]{1,0:T(8,128)(2,1)}, bf16[160,4096]{1,0:T(8,128)(2,1)}, u32[]{:S(2)}, u32[]{:S(2)}) collective-permute-start(bf16[160,4096]{1,0:T(8,128)(2,1)} %slice.20), channel_id=1, source_target_pairs={{32,8},{33,9},{34,10},{35,11},{36,12},{37,13},{38,14},{39,15},{64,... | collective-permute-start | bytes 3932168 | tf_op jit(solution)/shard_map/ppermute | solution.py:80
  64.7 13.7 %collective-permute-start.12 = (bf16[528,512]{1,0:T(8,128)(2,1)S(1)}, bf16[528,512]{1,0:T(8,128)(2,1)S(1)}, u32[]{:S(2)}, u32[]{:S(2)}) collective-permute-start(bf16[528,512]{1,0:T(8,128)(2,1)S(1)} %multiply_add_fusion), channel_id=1, source_target_pairs={{0,1},{32,33},{1,2},{33,34},{2,3},{34,35},{3,0},{35,32},{4,5},{36,... | collective-permute-start | bytes 1622024 | tf_op jit(solution)/shard_map/ppermute | solution.py:80
  64.9 12.3 %collective-permute-start.11 = (bf16[512,512]{1,0:T(8,128)(2,1)S(1)}, bf16[512,512]{1,0:T(8,128)(2,1)S(1)}, u32[]{:S(2)}, u32[]{:S(2)}) collective-permute-start(bf16[512,512]{1,0:T(8,128)(2,1)S(1)} %multiply_add_fusion.2), channel_id=1, source_target_pairs={{0,3},{32,35},{1,0},{33,32},{2,1},{34,33},{3,2},{35,34},{4,7},{36,... | collective-permute-start | bytes 1572872 | tf_op jit(solution)/shard_map/ppermute | solution.py:80
  78.4 12.4 %copy-start.14 = (bf16[528,512]{1,0:T(8,128)(2,1)}, bf16[528,512]{1,0:T(8,128)(2,1)S(1)}, u32[]{:S(2)}) copy-start(bf16[528,512]{1,0:T(8,128)(2,1)S(1)} %collective-permute-done.12.refs_17_) | copy-start | bytes 1622020
  81.9 16.4 %collective-permute-start.15 = (bf16[512,4096]{1,0:T(8,128)(2,1)}, bf16[512,4096]{1,0:T(8,128)(2,1)}, u32[]{:S(2)}, u32[]{:S(2)}) collective-permute-start(bf16[512,4096]{1,0:T(8,128)(2,1)} %refs_0_), channel_id=1, source_target_pairs={{0,32},{1,33},{2,34},{3,35},{4,36},{5,37},{6,38},{7,39},{96,64},{9... | collective-permute-start | bytes 12582920 | tf_op jit(solution)/shard_map/ppermute | solution.py:80
  83.2 15.1 %collective-permute-start.13 = (bf16[352,4096]{1,0:T(8,128)(2,1)}, bf16[352,4096]{1,0:T(8,128)(2,1)S(1)}, u32[]{:S(2)}, u32[]{:S(2)}) collective-permute-start(bf16[352,4096]{1,0:T(8,128)(2,1)} %collective-permute-done.3.refs_1_), channel_id=1, source_target_pairs={{32,0},{33,1},{34,2},{35,3},{36,4},{37,5},{38,6},{39,7},{64,96},{6... | collective-permute-start | bytes 8650760 | tf_op jit(solution)/shard_map/ppermute | solution.py:80
  88.4 9.9 %collective-permute-start.14 = (bf16[160,4096]{1,0:T(8,128)(2,1)}, bf16[160,4096]{1,0:T(8,128)(2,1)}, u32[]{:S(2)}, u32[]{:S(2)}) collective-permute-start(bf16[160,4096]{1,0:T(8,128)(2,1)} %collective-permute-done.10.refs_2_), channel_id=1, source_target_pairs={{32,0},{33,1},{34,2},{35,3},{36,4},{37,5},{38,6},{39,7},{64,96},{6... | collective-permute-start | bytes 3932168 | tf_op jit(solution)/shard_map/ppermute | solution.py:80
  (10 other events, 37.5 us)
